TPU v7x, 512 devices: a whole 4x4x16 slice. The times are simulated.
512 devices in a mesh: dp: 32 (over z, core), tensor: 16 (over y, x).
Axes of the slice: x: 4, y: 4, z: 16, core: 2. Of those that a mesh axis runs over, the one named last changes fastest.
Arguments:
- hidden: bfloat16 [8192, 4096], P(('dp', 'tensor')), may hold values from -3.6 to 3.6
- lengths: int32 [32, 32], P('dp'), may hold values from 1 to 80, 256 in all within a row
- positives: int32 [256], replicated, may hold values from 0 to 767, as said below
- negatives: int32 [256, 7], replicated, may hold values from 1 to 766, as said below
- in_gain: float32 [4096], replicated, may hold values from 0.25 to 1.75
- wq: bfloat16 [4096, 2048], P(None, 'tensor'), may hold values from -0.09375 to 0.09375
- wkv: bfloat16 [4096, 2048], P(None, 'tensor'), may hold values from -0.09375 to 0.09375
- q_gain: float32 [128], replicated, may hold values from 0.25 to 1.75
- k_gain: float32 [128], replicated, may hold values from 0.25 to 1.75
- wo: bfloat16 [2048, 4096], P('tensor'), may hold values from -0.125 to 0.125
- out_gain: float32 [4096], replicated, may hold values from 0.25 to 1.75
Outputs:
- d_hidden: bfloat16 [8192, 4096], P(('dp', 'tensor'))
- loss: float32 [], replicated
Inputs may be any that keep to these rules, and one draw needn't show every extreme that they name: Each group's 32 lengths sum to 256, and one of them is exactly 80. The 256 positives are distinct passages. The 7 hard negatives of a query are distinct, and none of them is any query's positive.
All inputs are finite; a program needn't handle non-finite values.
Results may differ from a plain program's by a relative error of at most 0.023.
Values may be sent and summed in bfloat16 or wider, within the bound.
No kernel may reach another device: no remote copies, remote signals or barrier semaphores. Data moves between devices by JAX's collectives and lax.ppermute only.
A program may use at most 64 MiB of HBM per device.

v0:
```python
import math
import jax
import jax.numpy as jnp
from jax import lax
from jax.sharding import PartitionSpec as P

QDEV = 8
EPSILON = 1e-06
SOFTMAX_TEMPER = 0.05
LOSS_MULTIPLIER = 8192.0
ROPE_BASE = 1000000.0


def swapped(value, axis, apart):
    mask = 2**apart
    pairs = [(source, source ^ mask) for source in range(lax.axis_size(axis))]
    return lax.ppermute(value, axis, pairs)


def rms_scale(tensor):
    return lax.rsqrt(jnp.mean(tensor * tensor, axis=-1, keepdims=True) + EPSILON)


def rope_tables(position, head_width):
    halfway = head_width // 2
    frequency = ROPE_BASE ** (-(jnp.arange(halfway, dtype=jnp.float32) * (2.0 / head_width)))
    angles = position[:, None] * frequency[None, :]
    angles = jnp.concatenate([angles, angles], axis=-1)
    return (jnp.cos(angles), jnp.sin(angles))


def rotate(tensor, cosine, sine):
    halfway = tensor.shape[-1] // 2
    turned = jnp.concatenate([-tensor[..., halfway:], tensor[..., :halfway]], axis=-1)
    return tensor * cosine + turned * sine


def segment_layout(lengths_row, total_tokens):
    seq_ends = jnp.cumsum(lengths_row)
    starts = seq_ends - lengths_row
    token_index = jnp.arange(total_tokens, dtype=jnp.int32)
    inside = (token_index[:, None] >= starts[None, :]) & (token_index[:, None] < seq_ends[None, :])
    offset = jnp.sum(jnp.where(inside, starts[None, :], 0), axis=1)
    position = (token_index - offset).astype(jnp.float32)
    return (inside, position, seq_ends - 1)


def head_forward(raw, gain, cosine, sine):
    inverse = rms_scale(raw)
    unit_form = raw * inverse
    return (unit_form, inverse, rotate(unit_form * gain, cosine, sine))


def norm_backward(grad, unit_form, inverse, gain):
    scaled = grad * gain
    return inverse * (scaled - unit_form * jnp.mean(unit_form * scaled, axis=-1, keepdims=True))


def head_backward(grad_rot, unit_form, inverse, gain, cosine, sine):
    return norm_backward(rotate(grad_rot, cosine, -sine), unit_form, inverse, gain)


def exchange(blocks, axis):
    return lax.all_to_all(blocks, axis, 0, 0, tiled=True)


def gather_rows(rows, axis):
    count = lax.axis_size(axis)
    copies = jnp.broadcast_to(rows[None], (count,) + rows.shape)
    return exchange(copies, axis)


def to_lanes(block, lanes):
    rows, width = block.shape
    return block.reshape(rows, width // lanes, lanes).reshape(-1, lanes)


def split16(value):
    parts = []
    rest = value
    for _ in range(3):
        part = rest.astype(jnp.bfloat16)
        parts.append(part)
        rest = rest - part.astype(jnp.float32)
    return parts


def contrast(scaled16, out_gain, positives, negatives):
    groups, sequences, width = scaled16.shape
    tensor_count = lax.axis_size("tensor")
    query_rows = scaled16[:, :QDEV].reshape(groups * QDEV, width)
    passage_rows = scaled16[:, QDEV:].reshape(-1, width)
    query_count, passage_count = (query_rows.shape[0], passage_rows.shape[0])
    own_queries = query_count // tensor_count
    features = width * tensor_count
    raw = jnp.dot(query_rows, passage_rows.T, preferred_element_type=jnp.float32)
    rows32 = jnp.concatenate([query_rows, passage_rows]).astype(jnp.float32)
    plain = rows32 / out_gain
    squares = jnp.sum(rows32 * rows32 + plain * plain * (EPSILON / features), axis=1)
    lanes = 128
    logit_rows = own_queries * passage_count // lanes
    packed = jnp.concatenate(
        [
            raw.reshape(tensor_count, own_queries, passage_count // lanes, lanes).reshape(
                tensor_count, logit_rows, lanes
            ),
            jnp.broadcast_to(
                squares.reshape(1, -1, lanes), (tensor_count, squares.shape[0] // lanes, lanes)
            ),
        ],
        axis=1,
    )
    summed = jnp.sum(exchange(packed, "tensor"), axis=0)
    inverse = lax.rsqrt(summed[logit_rows:].reshape(-1) + EPSILON * EPSILON)
    own = lax.axis_index("tensor") * own_queries
    inverse_query = lax.dynamic_slice_in_dim(inverse[:query_count], own, own_queries)
    inverse_passage = inverse[query_count:]
    logits = (
        summed[:logit_rows].reshape(own_queries, passage_count)
        * inverse_query[:, None]
        * inverse_passage[None, :]
        / SOFTMAX_TEMPER
    )
    passage_ids = jnp.arange(passage_count, dtype=jnp.int32)
    any_positive = jnp.any(positives[:, None] == passage_ids[None, :], axis=0)
    own_positives = lax.dynamic_slice_in_dim(positives, own, own_queries)
    own_negatives = lax.dynamic_slice_in_dim(negatives, own, own_queries)
    positive_hot = own_positives[:, None] == passage_ids[None, :]
    hard_hot = jnp.any(own_negatives[:, :, None] == passage_ids[None, None, :], axis=1)
    permitted_mask = any_positive[None, :] | hard_hot
    weight_params = jnp.where(permitted_mask, jnp.exp(logits - 1.0 / SOFTMAX_TEMPER), 0.0)
    totals = jnp.sum(weight_params, axis=1, keepdims=True)
    target_labels = jnp.sum(jnp.where(positive_hot, logits, 0.0), axis=1)
    loss_part = jnp.sum(jnp.log(totals[:, 0]) + 1.0 / SOFTMAX_TEMPER - target_labels)
    scaling_factor = LOSS_MULTIPLIER / (query_count * SOFTMAX_TEMPER)
    coef16 = (scaling_factor * (weight_params / totals - positive_hot.astype(jnp.float32))).astype(
        jnp.bfloat16
    )
    weighted = coef16.astype(jnp.float32) * logits * SOFTMAX_TEMPER
    along_query = jnp.sum(weighted, axis=1)
    along_passage = jnp.sum(weighted, axis=0)
    small = jnp.concatenate(
        [
            along_passage,
            jnp.pad(jnp.concatenate([along_query, loss_part[None]]), (0, lanes - own_queries - 1)),
        ]
    ).reshape(-1, lanes)
    small_rows = small.shape[0]
    sent = jnp.concatenate([coef16.reshape(-1, lanes)] + split16(small))
    pad = -sent.shape[0] % 16
    sent = jnp.pad(sent, ((0, pad), (0, 0)))
    arrived = gather_rows(sent, "tensor").reshape(tensor_count, -1, lanes)
    coef_all = arrived[:, :logit_rows].reshape(query_count, passage_count)
    parts = arrived[:, logit_rows : logit_rows + 3 * small_rows].astype(jnp.float32)
    small_all = jnp.sum(parts.reshape(tensor_count, 3, small_rows, lanes), axis=1)
    along_passage = jnp.sum(small_all[:, : small_rows - 1], axis=0).reshape(-1)
    along_query = small_all[:, small_rows - 1, :own_queries].reshape(-1)
    loss = jnp.sum(small_all[:, small_rows - 1, own_queries]) / query_count
    embeds16 = (rows32 * inverse[:, None]).astype(jnp.bfloat16)
    d_queries = jnp.dot(coef_all, embeds16[query_count:], preferred_element_type=jnp.float32)
    d_passages = jnp.dot(coef_all.T, embeds16[:query_count], preferred_element_type=jnp.float32)
    own_group = lax.axis_index("dp")
    others = sequences - QDEV

    def own_part(of_queries, of_passages):
        return jnp.concatenate(
            [
                lax.dynamic_slice_in_dim(of_queries, own_group * QDEV, QDEV),
                lax.dynamic_slice_in_dim(of_passages, own_group * others, others),
            ]
        )

    return (
        loss,
        own_part(d_queries, d_passages),
        own_part(along_query, along_passage),
        own_part(inverse[:query_count], inverse_passage),
    )


def on_device(
    hidden, lengths, positives, negatives, in_gain, wq, wkv, q_gain, k_gain, wo, out_gain
):
    tensor_count = lax.axis_size("tensor")
    tensor_index = lax.axis_index("tensor")
    own_rows, features = hidden.shape
    tokens_count = own_rows * tensor_count
    head_width = wq.shape[1]
    sequences = lengths.shape[1]
    chunk = features // tensor_count
    root = math.sqrt(head_width)
    is_even = tensor_index % 2 == 0
    hidden32 = hidden.astype(jnp.float32)
    inverse_in = rms_scale(hidden32)
    normed = (hidden32 * inverse_in * in_gain).astype(jnp.bfloat16)
    piece = gather_rows(normed, "tensor").reshape(tokens_count, features)
    own_index = tensor_index * own_rows + jnp.arange(own_rows, dtype=jnp.int32)
    inside, position, last = segment_layout(lengths[0], tokens_count)
    own_last = (last[:, None] == own_index[None, :]).astype(jnp.bfloat16)
    token_index = jnp.arange(tokens_count, dtype=jnp.int32)
    chosen = (last[:, None] == token_index[None, :]).astype(jnp.bfloat16)
    kv_own = jnp.dot(piece, wkv, preferred_element_type=jnp.float32)
    kv_other = swapped(kv_own, "tensor", 0)
    last_rows = jnp.dot(chosen, piece, preferred_element_type=jnp.float32).astype(jnp.bfloat16)
    query_raw = jnp.dot(last_rows, wq, preferred_element_type=jnp.float32)
    key_raw = jnp.where(is_even, kv_own, kv_other)
    value16 = jnp.where(is_even, kv_other, kv_own).astype(jnp.bfloat16)
    cos_key, sin_key = rope_tables(position, head_width)
    key_unit, key_inverse, key_rot = head_forward(key_raw, k_gain, cos_key, sin_key)
    key16 = key_rot.astype(jnp.bfloat16)
    cos_query, sin_query = rope_tables((lengths[0] - 1).astype(jnp.float32), head_width)
    query_unit, query_inverse, query_rot = head_forward(query_raw, q_gain, cos_query, sin_query)
    query16 = query_rot.astype(jnp.bfloat16)
    shift = root * jnp.max(q_gain) * jnp.max(k_gain)
    scores = jnp.dot(query16, key16.T, preferred_element_type=jnp.float32) / root
    weight_params = jnp.where(inside.T, jnp.exp(scores - shift), 0.0)
    probs = weight_params / jnp.sum(weight_params, axis=-1, keepdims=True)
    probs16 = probs.astype(jnp.bfloat16)
    attn16 = jnp.dot(probs16, value16, preferred_element_type=jnp.float32).astype(jnp.bfloat16)
    partial_rows = jnp.dot(attn16, wo, preferred_element_type=jnp.float32) + jnp.dot(
        own_last, hidden, preferred_element_type=jnp.float32
    )
    blocks = partial_rows.astype(jnp.bfloat16).reshape(sequences, tensor_count, chunk)
    arrived = exchange(blocks.transpose(1, 0, 2), "tensor")
    resid = jnp.sum(arrived.astype(jnp.float32), axis=0)
    own_gain = lax.dynamic_slice_in_dim(out_gain, tensor_index * chunk, chunk)
    scaled = resid * own_gain
    everyone = lax.all_gather(scaled.astype(jnp.bfloat16), "dp", axis=0, tiled=True)
    groups = lax.axis_size("dp")
    loss, d_embed, along, inverse = contrast(
        everyone.reshape(groups, sequences, chunk), own_gain, positives, negatives
    )
    inverse, along = (inverse[:, None], along[:, None])
    d_resid = inverse * own_gain * (d_embed - scaled * inverse * along) - resid * (
        along * inverse * inverse * (EPSILON / features)
    )
    d_resid16 = gather_rows(d_resid.astype(jnp.bfloat16), "tensor")
    d_resid16 = d_resid16.reshape(tensor_count, sequences, chunk)
    d_resid16 = d_resid16.transpose(1, 0, 2).reshape(sequences, features)
    d_attn16 = jnp.dot(d_resid16, wo.T, preferred_element_type=jnp.float32).astype(jnp.bfloat16)
    d_probs = jnp.dot(d_attn16, value16.T, preferred_element_type=jnp.float32)
    d_scores16 = (
        probs * (d_probs - jnp.sum(probs * d_probs, axis=-1, keepdims=True)) / root
    ).astype(jnp.bfloat16)
    d_query_rot = jnp.dot(d_scores16, key16, preferred_element_type=jnp.float32)
    d_key_rot = jnp.dot(d_scores16.T, query16, preferred_element_type=jnp.float32)
    d_value = jnp.dot(probs16.T, d_attn16, preferred_element_type=jnp.float32)
    d_key_raw = head_backward(d_key_rot, key_unit, key_inverse, k_gain, cos_key, sin_key)
    d_query_raw = head_backward(
        d_query_rot, query_unit, query_inverse, q_gain, cos_query, sin_query
    )
    mine = jnp.where(is_even, d_key_raw, d_value)
    theirs = jnp.where(is_even, d_value, d_key_raw)
    column16 = (mine + swapped(theirs, "tensor", 0)).astype(jnp.bfloat16)
    spread16 = jnp.dot(
        chosen.T, d_query_raw.astype(jnp.bfloat16), preferred_element_type=jnp.float32
    ).astype(jnp.bfloat16)
    product = jnp.dot(column16, wkv.T, preferred_element_type=jnp.float32) + jnp.dot(
        spread16, wq.T, preferred_element_type=jnp.float32
    )
    terms = exchange(product.astype(jnp.bfloat16), "tensor")
    d_normed = jnp.sum(terms.reshape(tensor_count, own_rows, features).astype(jnp.float32), axis=0)
    d_hidden = norm_backward(d_normed, hidden32 * inverse_in, inverse_in, in_gain)
    d_hidden = d_hidden + jnp.dot(own_last.T, d_resid16, preferred_element_type=jnp.float32)
    return (d_hidden.astype(jnp.bfloat16), loss)


def solution(mesh):
    placed = (
        P(("dp", "tensor"), None),
        P("dp", None),
        P(),
        P(),
        P(),
        P(None, "tensor"),
        P(None, "tensor"),
        P(),
        P(),
        P("tensor", None),
        P(),
    )
    return jax.shard_map(
        on_device,
        mesh=mesh,
        in_specs=placed,
        out_specs=(P(("dp", "tensor"), None), P()),
        check_vma=False,
    )
```

profile of v0, /device:TPU:2, one launch (start us, length us, event | category | flops | bytes accessed | tf_op | source)
XLA Modules:
  0.0 216.7 jit_solution(15755054820013921453)
XLA Ops:
  0.6 1.1 fusion.24
  1.8 0.5 copy-done.37
  2.3 1.0 fusion.20
  3.3 1.6 broadcast_in_dim.31
  4.9 9.6 %all-to-all-start = ((bf16[16,16,4096]{2,1,0:T(8,128)(2,1)}), bf16[16,16,4096]{2,1,0:T(8,128)(2,1)S(1)}, u32[]{:S(2)}, u32[]{:S(2)}) async-start(bf16[16,16,4096]{2,1,0:T(8,128)(2,1)} %broadcast_in_dim.31), calls=%async_computation | async-start | bytes 4194304 | tf_op jit(solution)/shard_map/all_to_all | solution.py:64
  14.5 0.6 reduce_max.19
  15.1 0.6 reduce_max.18
  17.5 1.1 fusion.53
  18.6 21.2 %all-to-all-done = bf16[16,16,4096]{2,1,0:T(8,128)(2,1)S(1)} async-done(((bf16[16,16,4096]{2,1,0:T(8,128)(2,1)}), bf16[16,16,4096]{2,1,0:T(8,128)(2,1)S(1)}, u32[]{:S(2)}, u32[]{:S(2)}) %all-to-all-start) | async-done | bytes 2097184 | tf_op jit(solution)/shard_map/all_to_all | solution.py:64
  39.8 2.0 multiply_reduce_fusion.6
  41.8 0.8 fusion.88
  42.7 4.8 %collective-permute-start = (f32[256,128]{0,1:T(8,128)S(1)}, f32[256,128]{0,1:T(8,128)S(1)}, u32[]{:S(2)}, u32[]{:S(2)}) collective-permute-start(f32[256,128]{0,1:T(8,128)S(1)} %fusion.88), channel_id=1, source_target_pairs={{0,1},{1,0},{2,3},{3,2},{4,5},{5,4},{6,7},{7,6},{8,9},{9,8},{10,11... | collective-permute-start | bytes 393224 | tf_op jit(solution)/shard_map/ppermute | solution.py:17
  47.8 2.6 %collective-permute-done = f32[256,128]{0,1:T(8,128)S(1)} collective-permute-done((f32[256,128]{0,1:T(8,128)S(1)}, f32[256,128]{0,1:T(8,128)S(1)}, u32[]{:S(2)}, u32[]{:S(2)}) %collective-permute-start) | collective-permute-done | bytes 131104 | tf_op jit(solution)/shard_map/ppermute | solution.py:17
  50.6 0.5 fusion.34
  51.1 0.6 copy-done.16
  52.1 0.5 fusion.1
  52.5 0.7 copy.44
  53.3 5.3 %all-to-all-start.1 = ((bf16[16,32,256]{2,1,0:T(8,128)(2,1)}), bf16[16,32,256]{2,1,0:T(8,128)(2,1)S(1)}, u32[]{:S(2)}, u32[]{:S(2)}) async-start(bf16[16,32,256]{2,1,0:T(8,128)(2,1)} %bitcast.79), calls=%async_computation.1 | async-start | bytes 524288 | tf_op jit(solution)/shard_map/all_to_all | solution.py:64
  58.6 0.8 dynamic_slice.30
  59.4 6.7 %all-to-all-done.1 = bf16[16,32,256]{2,1,0:T(8,128)(2,1)S(1)} async-done(((bf16[16,32,256]{2,1,0:T(8,128)(2,1)}), bf16[16,32,256]{2,1,0:T(8,128)(2,1)S(1)}, u32[]{:S(2)}, u32[]{:S(2)}) %all-to-all-start.1) | async-done | bytes 262176 | tf_op jit(solution)/shard_map/all_to_all | solution.py:64
  66.1 39.5 %all_gather.3 = bf16[1024,256]{1,0:T(8,128)(2,1)S(1)} all-gather(bf16[32,256]{1,0:T(8,128)(2,1)S(1)} %multiply_convert_fusion.3), channel_id=1, replica_groups=mesh['dp'=32,'tensor'=16] {'dp'}, dimensions={0}, use_global_device_ids=true | all-gather | bytes 540672 | tf_op jit(solution)/shard_map/all_gather | solution.py:228
  105.6 0.3 fusion.84
  105.9 0.3 copy-done.5
  106.2 0.3 fusion.9
  106.5 0.9 reshape_reshape.3
  107.5 2.1 pad_maximum_fusion
  109.6 4.9 %all-to-all-start.2 = ((f32[16,104,128]{2,1,0:T(8,128)}), f32[16,104,128]{2,1,0:T(8,128)S(1)}, u32[]{:S(2)}, u32[]{:S(2)}) async-start(f32[16,104,128]{2,1,0:T(8,128)} %pad_maximum_fusion), calls=%async_computation.2 | async-start | bytes 1703936 | tf_op jit(solution)/shard_map/all_to_all | solution.py:64
  114.6 0.6 eq.105
  115.5 0.6 reduce_or.22
  116.3 0.6 or.21
  116.9 0.6 eq.111
  117.6 11.6 %all-to-all-done.2 = f32[16,104,128]{2,1,0:T(8,128)S(1)} async-done(((f32[16,104,128]{2,1,0:T(8,128)}), f32[16,104,128]{2,1,0:T(8,128)S(1)}, u32[]{:S(2)}, u32[]{:S(2)}) %all-to-all-start.2) | async-done | bytes 852000 | tf_op jit(solution)/shard_map/all_to_all | solution.py:64
  129.5 0.9 fusion.51
  130.9 1.0 multiply_reduce_fusion.2
  132.3 0.6 subtract_reduce_fusion
  133.0 0.7 fusion.81
  133.7 0.8 multiply_reduce_fusion.3
  134.5 0.9 broadcast_in_dim.40
  135.5 5.6 %all-to-all-start.3 = ((bf16[16,128,128]{2,1,0:T(8,128)(2,1)}), bf16[16,128,128]{2,1,0:T(8,128)(2,1)}, u32[]{:S(2)}, u32[]{:S(2)}) async-start(bf16[16,128,128]{2,1,0:T(8,128)(2,1)} %broadcast_in_dim.40), calls=%async_computation.3 | async-start | bytes 1048576 | tf_op jit(solution)/shard_map/all_to_all | solution.py:64
  141.1 0.7 dynamic_slice.31
  141.7 0.6 dynamic_slice.32
  142.5 8.9 %all-to-all-done.3 = bf16[16,128,128]{2,1,0:T(8,128)(2,1)} async-done(((bf16[16,128,128]{2,1,0:T(8,128)(2,1)}), bf16[16,128,128]{2,1,0:T(8,128)(2,1)}, u32[]{:S(2)}, u32[]{:S(2)}) %all-to-all-start.3) | async-done | bytes 524320 | tf_op jit(solution)/shard_map/all_to_all | solution.py:64
  151.4 0.9 slice.105
  152.4 0.6 slice_reduce_fusion
  153.0 0.6 slice.106
  153.6 1.0 slice.102
  154.6 0.4 reshape.336
  155.1 0.3 fusion.14
  155.3 1.2 fusion.25
  156.8 0.7 dynamic_slice.39
  157.5 0.7 constant_dynamic-slice_fusion
  158.5 11.6 %all_to_all.34 = bf16[16,32,256]{2,1,0:T(8,128)(2,1)S(1)} all-to-all(bf16[16,32,256]{2,1,0:T(8,128)(2,1)S(1)} %broadcast_in_dim.41), channel_id=1, replica_groups=mesh['dp'=32,'tensor'=16] {'tensor'}, dimensions={0} | all-to-all | bytes 524288 | tf_op jit(solution)/shard_map/all_to_all | solution.py:64
  170.1 0.4 convolution_convert_fusion.2
  171.4 0.2 multiply_reduce_fusion.5
  171.7 0.5 multiply_reduce_fusion
  172.5 3.4 %collective-permute-start.1 = (f32[256,128]{0,1:T(8,128)S(1)}, f32[256,128]{0,1:T(8,128)S(1)}, u32[]{:S(2)}, u32[]{:S(2)}) collective-permute-start(f32[256,128]{0,1:T(8,128)S(1)} %get-tuple-element.39), channel_id=1, source_target_pairs={{0,1},{1,0},{2,3},{3,2},{4,5},{5,4},{6,7},{7,6},{8,9},{9,8},{10,11... | collective-permute-start | bytes 393224 | tf_op jit(solution)/shard_map/ppermute | solution.py:17
  175.9 4.1 %fusion.4 = f32[256,4096]{1,0:T(8,128)} fusion(bf16[4096,128]{1,0:T(8,128)(2,1)} %param.16, s32[32]{0:T(128)S(1)} %copy-done.31, f32[32,128]{1,0:T(8,128)S(1)} %get-tuple-element.7, f32[32,128]{1,0:T(8,128)S(1)} %get-tuple-element.34, f32[32]{0:T(128)S(1)} %broadcast_multiply_fusion.3, f32[32]{0:T(128)S(1)} %copy-done.34), kind=kOutput, calls=%fused_computation.13 | convolution fusion | flops 270594048 | bytes 5276032 | tf_op jit(solution)/shard_map/dot_general | solution.py:258
  180.0 4.3 %fusion = bf16[256,4096]{1,0:T(8,128)(2,1)} fusion(f32[256,4096]{1,0:T(8,128)} %fusion.4, bf16[4096,128]{1,0:T(8,128)(2,1)S(1)} %copy-done, f32[256,128]{0,1:T(8,128)S(1)} %collective-permute-done.1, f32[256,128]{0,1:T(8,128)S(1)} %get-tuple-element.40, pred[]{:T(512)S(6)} %eq.91, f32[256,128]{0,1:T(8,128)S(1)} %get-tuple-element.5, ...), kind=kOutput, calls=%fused_computation.1 | convolution fusion | flops 270761984 | bytes 7866369 | tf_op jit(solution)/shard_map/dot_general | solution.py:258
  184.2 4.4 %all-to-all-start.5 = ((bf16[16,16,4096]{2,1,0:T(8,128)(2,1)}), bf16[16,16,4096]{2,1,0:T(8,128)(2,1)S(1)}, u32[]{:S(2)}, u32[]{:S(2)}) async-start(bf16[16,16,4096]{2,1,0:T(8,128)(2,1)} %bitcast.18), calls=%async_computation.5 | async-start | bytes 4194304 | tf_op jit(solution)/shard_map/all_to_all | solution.py:64
  188.6 1.4 slice_reduce_fusion.1
  190.7 23.1 %all-to-all-done.5 = bf16[16,16,4096]{2,1,0:T(8,128)(2,1)S(1)} async-done(((bf16[16,16,4096]{2,1,0:T(8,128)(2,1)}), bf16[16,16,4096]{2,1,0:T(8,128)(2,1)S(1)}, u32[]{:S(2)}, u32[]{:S(2)}) %all-to-all-start.5) | async-done | bytes 2097184 | tf_op jit(solution)/shard_map/all_to_all | solution.py:64
  213.7 0.3 convert_reduce_fusion
  214.1 0.3 copy-done.38
  214.6 1.0 fusion.2
  (175 shorter events, 5.0 us)
Async XLA Ops:
  0.6 41.2 %copy-start = (bf16[4096,128]{1,0:T(8,128)(2,1)S(1)}, bf16[4096,128]{1,0:T(8,128)(2,1)}, u32[]{:S(2)}) copy-start(bf16[4096,128]{1,0:T(8,128)(2,1)} %param.17) | copy-start | bytes 3145732
  1.8 0.5 copy-start.37
  4.9 9.6 %copy-start.41 = (f32[128]{0:T(128)S(1)}, f32[128]{0:T(128)}, u32[]{:S(2)}) copy-start(f32[128]{0:T(128)} %param.19) | copy-start | bytes 1540
  4.9 10.2 %copy-start.35 = (f32[128]{0:T(128)S(1)}, f32[128]{0:T(128)}, u32[]{:S(2)}) copy-start(f32[128]{0:T(128)} %param.18) | copy-start | bytes 1540
  4.9 10.8 %copy-start.47 = (s32[1,32]{1,0:T(1,128)S(1)}, s32[1,32]{1,0:T(1,128)}, u32[]{:S(2)}) copy-start(s32[1,32]{1,0:T(1,128)} %param.12) | copy-start | bytes 388
  4.9 12.6 %copy-start.2 = (bf16[16,4096]{1,0:T(8,128)(2,1)S(1)}, bf16[16,4096]{1,0:T(8,128)(2,1)}, u32[]{:S(2)}) copy-start(bf16[16,4096]{1,0:T(8,128)(2,1)} %param.11) | copy-start | bytes 393220
  4.9 34.9 %all-to-all-start = ((bf16[16,16,4096]{2,1,0:T(8,128)(2,1)}), bf16[16,16,4096]{2,1,0:T(8,128)(2,1)S(1)}, u32[]{:S(2)}, u32[]{:S(2)}) async-start(bf16[16,16,4096]{2,1,0:T(8,128)(2,1)} %broadcast_in_dim.31), calls=%async_computation | async-start | bytes 4194304 | tf_op jit(solution)/shard_map/all_to_all | solution.py:64
  17.3 25.4 %copy-start.43 = (s32[16]{0:T(128)}, s32[16]{0:T(128)S(1)}, u32[]{:S(2)}) copy-start(s32[16]{0:T(128)S(1)} %iota_add_fusion) | copy-start | bytes 196
  17.4 25.3 %copy-start.30 = (s32[32]{0:T(128)}, s32[32]{0:T(128)S(1)}, u32[]{:S(2)}) copy-start(s32[32]{0:T(128)S(1)} %broadcast_add_fusion) | copy-start | bytes 388
  17.5 33.1 %copy-start.7 = (f32[256,64]{0,1:T(8,128)}, f32[256,64]{0,1:T(8,128)S(1)}, u32[]{:S(2)}) copy-start(f32[256,64]{0,1:T(8,128)S(1)} %broadcast_multiply_fusion) | copy-start | bytes 196612
  42.7 9.4 %copy-start.1 = (bf16[128,4096]{1,0:T(8,128)(2,1)S(1)}, bf16[128,4096]{1,0:T(8,128)(2,1)}, u32[]{:S(2)}) copy-start(bf16[128,4096]{1,0:T(8,128)(2,1)} %param.20) | copy-start | bytes 3145732
  42.7 9.4 %copy-start.4 = (f32[32,4096]{1,0:T(8,128)S(1)}, f32[32,4096]{1,0:T(8,128)}, u32[]{:S(2)}) copy-start(f32[32,4096]{1,0:T(8,128)} %fusion.53) | copy-start | bytes 1572868
  42.7 7.8 %copy-start.33 = (f32[32]{0:T(128)}, f32[32]{0:T(128)S(1)}, u32[]{:S(2)}) copy-start(f32[32]{0:T(128)S(1)} %add_rsqrt_fusion.1) | copy-start | bytes 388
  42.7 7.7 %collective-permute-start = (f32[256,128]{0,1:T(8,128)S(1)}, f32[256,128]{0,1:T(8,128)S(1)}, u32[]{:S(2)}, u32[]{:S(2)}) collective-permute-start(f32[256,128]{0,1:T(8,128)S(1)} %fusion.88), channel_id=1, source_target_pairs={{0,1},{1,0},{2,3},{3,2},{4,5},{5,4},{6,7},{7,6},{8,9},{9,8},{10,11... | collective-permute-start | bytes 393224 | tf_op jit(solution)/shard_map/ppermute | solution.py:17
  47.6 2.9 %copy-start.19 = (f32[32,64]{1,0:T(8,128)}, f32[32,64]{1,0:T(8,128)S(1)}, u32[]{:S(2)}) copy-start(f32[32,64]{1,0:T(8,128)S(1)} %get-tuple-element.41) | copy-start | bytes 24580
  47.8 5.5 %copy-start.24 = (bf16[32,128]{1,0:T(8,128)(2,1)}, bf16[32,128]{1,0:T(8,128)(2,1)S(1)}, u32[]{:S(2)}) copy-start(bf16[32,128]{1,0:T(8,128)(2,1)S(1)} %fusion.56) | copy-start | bytes 24580
  50.5 2.8 %copy-start.22 = (f32[256]{0:T(256)}, f32[256]{0:T(256)S(1)}, u32[]{:S(2)}) copy-start(f32[256]{0:T(256)S(1)} %add_rsqrt_fusion) | copy-start | bytes 3076
  51.1 0.6 copy-start.16
  52.0 53.6 %copy-start.9 = (f32[32,256]{1,0:T(8,128)}, f32[32,256]{1,0:T(8,128)S(1)}, u32[]{:S(2)}) copy-start(f32[32,256]{1,0:T(8,128)S(1)} %get-tuple-element.36) | copy-start | bytes 98308
  52.0 53.6 %copy-start.39 = (f32[32]{0:T(128)}, f32[32]{0:T(128)S(1)}, u32[]{:S(2)}) copy-start(f32[32]{0:T(128)S(1)} %get-tuple-element.35) | copy-start | bytes 388
  52.0 7.3 %copy-start.14 = (bf16[256,128]{0,1:T(8,128)(2,1)}, bf16[256,128]{0,1:T(8,128)(2,1)S(1)}, u32[]{:S(2)}) copy-start(bf16[256,128]{0,1:T(8,128)(2,1)S(1)} %select_convert_fusion) | copy-start | bytes 196612
  53.3 12.7 %all-to-all-start.1 = ((bf16[16,32,256]{2,1,0:T(8,128)(2,1)}), bf16[16,32,256]{2,1,0:T(8,128)(2,1)S(1)}, u32[]{:S(2)}, u32[]{:S(2)}) async-start(bf16[16,32,256]{2,1,0:T(8,128)(2,1)} %bitcast.79), calls=%async_computation.1 | async-start | bytes 524288 | tf_op jit(solution)/shard_map/all_to_all | solution.py:64
  59.3 48.1 %copy-start.27 = (f32[256]{0:T(256)}, f32[256]{0:T(256)S(1)}, u32[]{:S(2)}) copy-start(f32[256]{0:T(256)S(1)} %dynamic_slice.30) | copy-start | bytes 3076
  66.0 39.5 %copy-start.11 = (f32[32,256]{1,0:T(8,128)}, f32[32,256]{1,0:T(8,128)S(1)}, u32[]{:S(2)}) copy-start(f32[32,256]{1,0:T(8,128)S(1)} %convert_reduce_fusion.1) | copy-start | bytes 98308
  105.6 0.7 copy-start.5
  107.5 7.0 %copy-start.48 = (s32[256]{0:T(256)S(1)}, s32[256]{0:T(256)}, u32[]{:S(2)}) copy-start(s32[256]{0:T(256)} %param.13) | copy-start | bytes 3076
  107.5 7.8 %copy-start.46 = (s32[256,7]{0,1:T(8,128)S(1)}, s32[256,7]{0,1:T(8,128)}, u32[]{:S(2)}) copy-start(s32[256,7]{0,1:T(8,128)} %param.14) | copy-start | bytes 21508
  109.6 19.6 %all-to-all-start.2 = ((f32[16,104,128]{2,1,0:T(8,128)}), f32[16,104,128]{2,1,0:T(8,128)S(1)}, u32[]{:S(2)}, u32[]{:S(2)}) async-start(f32[16,104,128]{2,1,0:T(8,128)} %pad_maximum_fusion), calls=%async_computation.2 | async-start | bytes 1703936 | tf_op jit(solution)/shard_map/all_to_all | solution.py:64
  114.6 0.7 copy-start.45
  115.4 1.5 copy-start.21
  116.3 0.6 copy-start.29
  129.2 13.1 %copy-start.6 = (bf16[256,256]{1,0:T(8,128)(2,1)S(1)}, bf16[256,256]{1,0:T(8,128)(2,1)}, u32[]{:S(2)}) copy-start(bf16[256,256]{1,0:T(8,128)(2,1)} %copy-done.5) | copy-start | bytes 393220
  135.5 16.0 %all-to-all-start.3 = ((bf16[16,128,128]{2,1,0:T(8,128)(2,1)}), bf16[16,128,128]{2,1,0:T(8,128)(2,1)}, u32[]{:S(2)}, u32[]{:S(2)}) async-start(bf16[16,128,128]{2,1,0:T(8,128)(2,1)} %broadcast_in_dim.40), calls=%async_computation.3 | async-start | bytes 1048576 | tf_op jit(solution)/shard_map/all_to_all | solution.py:64
  152.4 0.6 copy-start.13
  155.0 1.5 copy-start.26
  155.0 3.2 %copy-start.49 = (f32[8]{0:T(128)S(1)}, f32[8]{0:T(128)}, u32[]{:S(2)}) copy-start(f32[8]{0:T(128)} %dynamic_slice.31) | copy-start | bytes 100
  155.0 3.2 %copy-start.50 = (f32[24]{0:T(128)S(1)}, f32[24]{0:T(128)}, u32[]{:S(2)}) copy-start(f32[24]{0:T(128)} %dynamic_slice.32) | copy-start | bytes 292
  155.0 3.3 %copy-start.12 = (f32[32,256]{1,0:T(8,128)S(1)}, f32[32,256]{1,0:T(8,128)}, u32[]{:S(2)}) copy-start(f32[32,256]{1,0:T(8,128)} %copy-done.11) | copy-start | bytes 98308
  155.0 3.3 %copy-start.28 = (f32[256]{0:T(256)S(1)}, f32[256]{0:T(256)}, u32[]{:S(2)}) copy-start(f32[256]{0:T(256)} %copy-done.27) | copy-start | bytes 3076
  155.3 15.2 %copy-start.10 = (f32[32,256]{1,0:T(8,128)S(1)}, f32[32,256]{1,0:T(8,128)}, u32[]{:S(2)}) copy-start(f32[32,256]{1,0:T(8,128)} %copy-done.9) | copy-start | bytes 98308
  156.5 14.1 %copy-start.15 = (bf16[256,128]{0,1:T(8,128)(2,1)S(1)}, bf16[256,128]{0,1:T(8,128)(2,1)}, u32[]{:S(2)}) copy-start(bf16[256,128]{0,1:T(8,128)(2,1)} %copy-done.14) | copy-start | bytes 196612
  156.5 14.1 %copy-start.40 = (f32[32]{0:T(128)S(1)}, f32[32]{0:T(128)}, u32[]{:S(2)}) copy-start(f32[32]{0:T(128)} %copy-done.39) | copy-start | bytes 388
  156.5 14.4 %copy-start.17 = (bf16[256,128]{0,1:T(8,128)(2,1)S(1)}, bf16[256,128]{0,1:T(8,128)(2,1)}, u32[]{:S(2)}) copy-start(bf16[256,128]{0,1:T(8,128)(2,1)} %copy-done.16) | copy-start | bytes 196612
  156.5 14.5 %copy-start.25 = (bf16[32,128]{1,0:T(8,128)(2,1)S(1)}, bf16[32,128]{1,0:T(8,128)(2,1)}, u32[]{:S(2)}) copy-start(bf16[32,128]{1,0:T(8,128)(2,1)} %copy-done.24) | copy-start | bytes 24580
  156.6 14.9 %copy-start.20 = (f32[32,64]{1,0:T(8,128)S(1)}, f32[32,64]{1,0:T(8,128)}, u32[]{:S(2)}) copy-start(f32[32,64]{1,0:T(8,128)} %copy-done.19) | copy-start | bytes 24580
  156.6 14.8 %copy-start.34 = (f32[32]{0:T(128)S(1)}, f32[32]{0:T(128)}, u32[]{:S(2)}) copy-start(f32[32]{0:T(128)} %copy-done.33) | copy-start | bytes 388
  156.6 14.8 %copy-start.36 = (f32[128]{0:T(128)S(1)}, f32[128]{0:T(128)}, u32[]{:S(2)}) copy-start(f32[128]{0:T(128)} %param.18) | copy-start | bytes 1540
  156.6 15.1 %copy-start.8 = (f32[256,64]{0,1:T(8,128)S(1)}, f32[256,64]{0,1:T(8,128)}, u32[]{:S(2)}) copy-start(f32[256,64]{0,1:T(8,128)} %copy-done.7) | copy-start | bytes 196612
  156.6 15.1 %copy-start.23 = (f32[256]{0:T(256)S(1)}, f32[256]{0:T(256)}, u32[]{:S(2)}) copy-start(f32[256]{0:T(256)} %copy-done.22) | copy-start | bytes 3076
  156.6 15.1 %copy-start.42 = (f32[128]{0:T(128)S(1)}, f32[128]{0:T(128)}, u32[]{:S(2)}) copy-start(f32[128]{0:T(128)} %param.19) | copy-start | bytes 1540
  170.1 5.8 %copy-start.31 = (s32[32]{0:T(128)S(1)}, s32[32]{0:T(128)}, u32[]{:S(2)}) copy-start(s32[32]{0:T(128)} %copy-done.30) | copy-start | bytes 388
  172.5 7.5 %collective-permute-start.1 = (f32[256,128]{0,1:T(8,128)S(1)}, f32[256,128]{0,1:T(8,128)S(1)}, u32[]{:S(2)}, u32[]{:S(2)}) collective-permute-start(f32[256,128]{0,1:T(8,128)S(1)} %get-tuple-element.39), channel_id=1, source_target_pairs={{0,1},{1,0},{2,3},{3,2},{4,5},{5,4},{6,7},{7,6},{8,9},{9,8},{10,11... | collective-permute-start | bytes 393224 | tf_op jit(solution)/shard_map/ppermute | solution.py:17
  184.2 29.5 %all-to-all-start.5 = ((bf16[16,16,4096]{2,1,0:T(8,128)(2,1)}), bf16[16,16,4096]{2,1,0:T(8,128)(2,1)S(1)}, u32[]{:S(2)}, u32[]{:S(2)}) async-start(bf16[16,16,4096]{2,1,0:T(8,128)(2,1)} %bitcast.18), calls=%async_computation.5 | async-start | bytes 4194304 | tf_op jit(solution)/shard_map/all_to_all | solution.py:64
  188.6 25.4 %copy-start.3 = (bf16[16,4096]{1,0:T(8,128)(2,1)S(1)}, bf16[16,4096]{1,0:T(8,128)(2,1)}, u32[]{:S(2)}) copy-start(bf16[16,4096]{1,0:T(8,128)(2,1)} %param.11) | copy-start | bytes 393220
  188.6 25.5 %copy-start.18 = (f32[4096]{0:T(1024)S(1)}, f32[4096]{0:T(1024)}, u32[]{:S(2)}) copy-start(f32[4096]{0:T(1024)} %param.15) | copy-start | bytes 49156
  213.7 0.6 copy-start.38
  213.7 0.8 copy-start.32
  213.7 0.8 copy-start.44
where the time goes:
time: 218 us; the launch traced here: 217 us
  waiting for transfers between devices  74.1 us (34%)
  blocking collectives  51.1 us (23%)
  starting transfers between devices  37.9 us (17%)
  matrix products  16.9 us (8%)
  local copies, waits for them, and re-layouts  16.2 us (7%)
  other arithmetic  15.9 us (7%)
  between operations  4.59 us (2%)
    all_to_all x5, waiting for transfers between devices, exchange(): return lax.all_to_all(blocks, axis, 0, 0, tiled=True)  71.5 us
    all_gather x1, blocking collectives, on_device(): lax.all_gather(scaled.astype(jnp.bfloat16), 'dp', axis=0, tiled=True)  39.5 us
    all_to_all x5, starting transfers between devices, exchange(): return lax.all_to_all(blocks, axis, 0, 0, tiled=True)  29.7 us
    all_to_all x1, blocking collectives, exchange(): return lax.all_to_all(blocks, axis, 0, 0, tiled=True)  11.6 us
    ppermute x2, starting transfers between devices, swapped(): return lax.ppermute(value, axis, pairs)  8.13 us
  transfers between devices with their start and end apart: 7, of which 6 were waited for; matrix products, arithmetic and copies ran while one was open for 6% of the time, Pallas kernels for 0%

commit v1 on v0

--- a/solution.py
+++ b/solution.py
@@ -181,6 +181,12 @@
 def on_device(
     hidden, lengths, positives, negatives, in_gain, wq, wkv, q_gain, k_gain, wo, out_gain
 ):
+
+    def mark_screen(panel, link_axis):
+        local_out = jnp.stack([panel for _ in range(lax.axis_size(link_axis))])
+        z1 = lax.all_to_all(local_out, axis_name=link_axis, split_axis=0, concat_axis=0)
+        return jnp.concatenate(z1, axis=0)
+
     tensor_count = lax.axis_size("tensor")
     tensor_index = lax.axis_index("tensor")
     own_rows, features = hidden.shape
@@ -225,7 +231,7 @@
     resid = jnp.sum(arrived.astype(jnp.float32), axis=0)
     own_gain = lax.dynamic_slice_in_dim(out_gain, tensor_index * chunk, chunk)
     scaled = resid * own_gain
-    everyone = lax.all_gather(scaled.astype(jnp.bfloat16), "dp", axis=0, tiled=True)
+    everyone = mark_screen(scaled.astype(jnp.bfloat16), "dp")
     groups = lax.axis_size("dp")
     loss, d_embed, along, inverse = contrast(
         everyone.reshape(groups, sequences, chunk), own_gain, positives, negatives

time: 218 us -> 230 us (1.055)
  the two profiles are of different devices: /device:TPU:2 before, /device:TPU:64 now
where the time goes in v1:
time: 230 us; the launch traced here: 228 us
  waiting for transfers between devices  91.2 us (40%)
  blocking collectives  56.3 us (24%)
  starting transfers between devices  26.8 us (12%)
  matrix products  16.9 us (7%)
  local copies, waits for them, and re-layouts  16.6 us (7%)
  other arithmetic  15.9 us (7%)
  between operations  4.69 us (2%)
    all_to_all x5, waiting for transfers between devices, exchange(): return lax.all_to_all(blocks, axis, 0, 0, tiled=True)  86.3 us
    all_to_all x1, blocking collectives, mark_screen(): lax.all_to_all(local_out, axis_name=link_axis, split_axis=0, concat_axis=0)  44.8 us
    all_to_all x5, starting transfers between devices, exchange(): return lax.all_to_all(blocks, axis, 0, 0, tiled=True)  22.3 us
    all_to_all x1, blocking collectives, exchange(): return lax.all_to_all(blocks, axis, 0, 0, tiled=True)  11.5 us
    ppermute x2, waiting for transfers between devices, swapped(): return lax.ppermute(value, axis, pairs)  4.9 us
  transfers between devices with their start and end apart: 7, of which 7 were waited for; matrix products, arithmetic and copies ran while one was open for 6% of the time, Pallas kernels for 0%

profile of v1, /device:TPU:64, one launch (start us, length us, event | category | flops | bytes accessed | tf_op | source)
XLA Modules:
  0.0 228.5 jit_solution(14501871206120959050)
XLA Ops:
  0.6 1.1 fusion.24
  1.8 0.5 copy-done.37
  2.3 1.0 fusion.20
  3.3 1.6 broadcast_in_dim.31
  4.9 7.2 %all-to-all-start = ((bf16[16,16,4096]{2,1,0:T(8,128)(2,1)}), bf16[16,16,4096]{2,1,0:T(8,128)(2,1)S(1)}, u32[]{:S(2)}, u32[]{:S(2)}) async-start(bf16[16,16,4096]{2,1,0:T(8,128)(2,1)} %broadcast_in_dim.31), calls=%async_computation | async-start | bytes 4194304 | tf_op jit(solution)/shard_map/all_to_all | solution.py:64
  12.1 0.6 reduce_max.19
  12.7 0.6 reduce_max.18
  15.2 1.1 fusion.53
  16.2 27.5 %all-to-all-done = bf16[16,16,4096]{2,1,0:T(8,128)(2,1)S(1)} async-done(((bf16[16,16,4096]{2,1,0:T(8,128)(2,1)}), bf16[16,16,4096]{2,1,0:T(8,128)(2,1)S(1)}, u32[]{:S(2)}, u32[]{:S(2)}) %all-to-all-start) | async-done | bytes 2097184 | tf_op jit(solution)/shard_map/all_to_all | solution.py:64
  43.8 2.0 multiply_reduce_fusion.6
  45.8 0.8 fusion.88
  46.7 2.1 collective-permute-start
  49.0 4.6 %collective-permute-done = f32[256,128]{0,1:T(8,128)S(1)} collective-permute-done((f32[256,128]{0,1:T(8,128)S(1)}, f32[256,128]{0,1:T(8,128)S(1)}, u32[]{:S(2)}, u32[]{:S(2)}) %collective-permute-start) | collective-permute-done | bytes 131104 | tf_op jit(solution)/shard_map/ppermute | solution.py:17
  53.9 0.5 fusion.34
  54.4 0.6 copy-done.16
  55.3 0.5 fusion.1
  55.8 0.7 copy.44
  56.5 3.6 %all-to-all-start.1 = ((bf16[16,32,256]{2,1,0:T(8,128)(2,1)}), bf16[16,32,256]{2,1,0:T(8,128)(2,1)S(1)}, u32[]{:S(2)}, u32[]{:S(2)}) async-start(bf16[16,32,256]{2,1,0:T(8,128)(2,1)} %bitcast.78), calls=%async_computation.1 | async-start | bytes 524288 | tf_op jit(solution)/shard_map/all_to_all | solution.py:64
  60.0 0.8 dynamic_slice.30
  60.8 7.9 %all-to-all-done.1 = bf16[16,32,256]{2,1,0:T(8,128)(2,1)S(1)} async-done(((bf16[16,32,256]{2,1,0:T(8,128)(2,1)}), bf16[16,32,256]{2,1,0:T(8,128)(2,1)S(1)}, u32[]{:S(2)}, u32[]{:S(2)}) %all-to-all-start.1) | async-done | bytes 262176 | tf_op jit(solution)/shard_map/all_to_all | solution.py:64
  68.9 44.8 %all_to_all.39 = bf16[32,32,256]{2,1,0:T(8,128)(2,1)S(1)} all-to-all(bf16[32,32,256]{2,1,0:T(8,128)(2,1)S(1)} %stack.2), channel_id=1, replica_groups=mesh['dp'=32,'tensor'=16] {'dp'}, dimensions={0} | all-to-all | bytes 1048576 | tf_op jit(solution)/shard_map/all_to_all | solution.py:187
  113.8 0.6 copy-done.5
  114.4 0.3 fusion.9
  114.7 0.3 fusion.84
  115.0 0.9 reshape_reshape.3
  115.9 2.1 pad_maximum_fusion
  118.1 3.6 %all-to-all-start.3 = ((f32[16,104,128]{2,1,0:T(8,128)}), f32[16,104,128]{2,1,0:T(8,128)S(1)}, u32[]{:S(2)}, u32[]{:S(2)}) async-start(f32[16,104,128]{2,1,0:T(8,128)} %pad_maximum_fusion), calls=%async_computation.3 | async-start | bytes 1703936 | tf_op jit(solution)/shard_map/all_to_all | solution.py:64
  121.9 0.6 eq.105
  122.7 0.6 reduce_or.22
  123.5 0.6 or.21
  124.1 0.6 eq.111
  124.8 14.3 %all-to-all-done.3 = f32[16,104,128]{2,1,0:T(8,128)S(1)} async-done(((f32[16,104,128]{2,1,0:T(8,128)}), f32[16,104,128]{2,1,0:T(8,128)S(1)}, u32[]{:S(2)}, u32[]{:S(2)}) %all-to-all-start.3) | async-done | bytes 852000 | tf_op jit(solution)/shard_map/all_to_all | solution.py:64
  139.4 0.9 fusion.51
  140.7 1.0 multiply_reduce_fusion.2
  142.2 0.6 subtract_reduce_fusion
  142.8 0.7 fusion.81
  143.6 0.8 multiply_reduce_fusion.3
  144.4 0.9 broadcast_in_dim.40
  145.3 4.2 %all-to-all-start.4 = ((bf16[16,128,128]{2,1,0:T(8,128)(2,1)}), bf16[16,128,128]{2,1,0:T(8,128)(2,1)}, u32[]{:S(2)}, u32[]{:S(2)}) async-start(bf16[16,128,128]{2,1,0:T(8,128)(2,1)} %broadcast_in_dim.40), calls=%async_computation.4 | async-start | bytes 1048576 | tf_op jit(solution)/shard_map/all_to_all | solution.py:64
  149.6 0.7 dynamic_slice.31
  150.3 0.6 dynamic_slice.32
  151.1 10.6 %all-to-all-done.4 = bf16[16,128,128]{2,1,0:T(8,128)(2,1)} async-done(((bf16[16,128,128]{2,1,0:T(8,128)(2,1)}), bf16[16,128,128]{2,1,0:T(8,128)(2,1)}, u32[]{:S(2)}, u32[]{:S(2)}) %all-to-all-start.4) | async-done | bytes 524320 | tf_op jit(solution)/shard_map/all_to_all | solution.py:64
  161.7 0.9 slice.105
  162.7 0.6 slice_reduce_fusion
  163.3 0.6 slice.106
  163.9 1.0 slice.102
  164.9 0.4 reshape.343
  165.3 0.3 fusion.14
  165.6 1.2 fusion.25
  167.0 0.7 dynamic_slice.39
  167.8 0.7 constant_dynamic-slice_fusion
  168.7 11.5 %all_to_all.40 = bf16[16,32,256]{2,1,0:T(8,128)(2,1)S(1)} all-to-all(bf16[16,32,256]{2,1,0:T(8,128)(2,1)S(1)} %broadcast_in_dim.41), channel_id=1, replica_groups=mesh['dp'=32,'tensor'=16] {'tensor'}, dimensions={0} | all-to-all | bytes 524288 | tf_op jit(solution)/shard_map/all_to_all | solution.py:64
  180.3 0.4 convolution_convert_fusion.2
  181.9 0.5 multiply_reduce_fusion
  182.6 2.5 %collective-permute-start.1 = (f32[256,128]{0,1:T(8,128)S(1)}, f32[256,128]{0,1:T(8,128)S(1)}, u32[]{:S(2)}, u32[]{:S(2)}) collective-permute-start(f32[256,128]{0,1:T(8,128)S(1)} %get-tuple-element.39), channel_id=1, source_target_pairs={{0,1},{1,0},{2,3},{3,2},{4,5},{5,4},{6,7},{7,6},{8,9},{9,8},{10,11... | collective-permute-start | bytes 393224 | tf_op jit(solution)/shard_map/ppermute | solution.py:17
  185.1 4.1 %fusion.4 = f32[256,4096]{1,0:T(8,128)} fusion(bf16[4096,128]{1,0:T(8,128)(2,1)} %param.16, s32[32]{0:T(128)S(1)} %copy-done.31, f32[32,128]{1,0:T(8,128)S(1)} %get-tuple-element.7, f32[32,128]{1,0:T(8,128)S(1)} %get-tuple-element.34, f32[32]{0:T(128)S(1)} %broadcast_multiply_fusion.3, f32[32]{0:T(128)S(1)} %copy-done.34), kind=kOutput, calls=%fused_computation.13 | convolution fusion | flops 270594048 | bytes 5276032 | tf_op jit(solution)/shard_map/dot_general | solution.py:264
  189.2 0.3 collective-permute-done.1
  189.5 4.3 %fusion = bf16[256,4096]{1,0:T(8,128)(2,1)} fusion(f32[256,4096]{1,0:T(8,128)} %fusion.4, bf16[4096,128]{1,0:T(8,128)(2,1)S(1)} %copy-done, f32[256,128]{0,1:T(8,128)S(1)} %collective-permute-done.1, f32[256,128]{0,1:T(8,128)S(1)} %get-tuple-element.40, pred[]{:T(512)S(6)} %eq.91, f32[256,128]{0,1:T(8,128)S(1)} %get-tuple-element.5, ...), kind=kOutput, calls=%fused_computation.1 | convolution fusion | flops 270761984 | bytes 7866369 | tf_op jit(solution)/shard_map/dot_general | solution.py:264
  193.8 3.7 %all-to-all-start.6 = ((bf16[16,16,4096]{2,1,0:T(8,128)(2,1)}), bf16[16,16,4096]{2,1,0:T(8,128)(2,1)S(1)}, u32[]{:S(2)}, u32[]{:S(2)}) async-start(bf16[16,16,4096]{2,1,0:T(8,128)(2,1)} %bitcast.17), calls=%async_computation.6 | async-start | bytes 4194304 | tf_op jit(solution)/shard_map/all_to_all | solution.py:64
  197.5 1.4 slice_reduce_fusion.1
  199.6 25.9 %all-to-all-done.6 = bf16[16,16,4096]{2,1,0:T(8,128)(2,1)S(1)} async-done(((bf16[16,16,4096]{2,1,0:T(8,128)(2,1)}), bf16[16,16,4096]{2,1,0:T(8,128)(2,1)S(1)}, u32[]{:S(2)}, u32[]{:S(2)}) %all-to-all-start.6) | async-done | bytes 2097184 | tf_op jit(solution)/shard_map/all_to_all | solution.py:64
  225.5 0.3 convert_reduce_fusion
  225.8 0.3 copy-done.38
  226.4 1.0 fusion.2
  (176 shorter events, 5.3 us)
Async XLA Ops:
  0.6 45.1 %copy-start = (bf16[4096,128]{1,0:T(8,128)(2,1)S(1)}, bf16[4096,128]{1,0:T(8,128)(2,1)}, u32[]{:S(2)}) copy-start(bf16[4096,128]{1,0:T(8,128)(2,1)} %param.17) | copy-start | bytes 3145732
  1.8 0.5 copy-start.37
  4.9 7.2 %copy-start.41 = (f32[128]{0:T(128)S(1)}, f32[128]{0:T(128)}, u32[]{:S(2)}) copy-start(f32[128]{0:T(128)} %param.19) | copy-start | bytes 1540
  4.9 7.8 %copy-start.35 = (f32[128]{0:T(128)S(1)}, f32[128]{0:T(128)}, u32[]{:S(2)}) copy-start(f32[128]{0:T(128)} %param.18) | copy-start | bytes 1540
  4.9 8.4 %copy-start.47 = (s32[1,32]{1,0:T(1,128)S(1)}, s32[1,32]{1,0:T(1,128)}, u32[]{:S(2)}) copy-start(s32[1,32]{1,0:T(1,128)} %param.12) | copy-start | bytes 388
  4.9 10.2 %copy-start.2 = (bf16[16,4096]{1,0:T(8,128)(2,1)S(1)}, bf16[16,4096]{1,0:T(8,128)(2,1)}, u32[]{:S(2)}) copy-start(bf16[16,4096]{1,0:T(8,128)(2,1)} %param.11) | copy-start | bytes 393220
  4.9 38.8 %all-to-all-start = ((bf16[16,16,4096]{2,1,0:T(8,128)(2,1)}), bf16[16,16,4096]{2,1,0:T(8,128)(2,1)S(1)}, u32[]{:S(2)}, u32[]{:S(2)}) async-start(bf16[16,16,4096]{2,1,0:T(8,128)(2,1)} %broadcast_in_dim.31), calls=%async_computation | async-start | bytes 4194304 | tf_op jit(solution)/shard_map/all_to_all | solution.py:64
  14.9 31.7 %copy-start.43 = (s32[16]{0:T(128)}, s32[16]{0:T(128)S(1)}, u32[]{:S(2)}) copy-start(s32[16]{0:T(128)S(1)} %iota_add_fusion) | copy-start | bytes 196
  15.1 31.6 %copy-start.30 = (s32[32]{0:T(128)}, s32[32]{0:T(128)S(1)}, u32[]{:S(2)}) copy-start(s32[32]{0:T(128)S(1)} %broadcast_add_fusion) | copy-start | bytes 388
  15.2 38.7 %copy-start.7 = (f32[256,64]{0,1:T(8,128)}, f32[256,64]{0,1:T(8,128)S(1)}, u32[]{:S(2)}) copy-start(f32[256,64]{0,1:T(8,128)S(1)} %broadcast_multiply_fusion) | copy-start | bytes 196612
  46.6 8.7 %copy-start.1 = (bf16[128,4096]{1,0:T(8,128)(2,1)S(1)}, bf16[128,4096]{1,0:T(8,128)(2,1)}, u32[]{:S(2)}) copy-start(bf16[128,4096]{1,0:T(8,128)(2,1)} %param.20) | copy-start | bytes 3145732
  46.6 8.7 %copy-start.4 = (f32[32,4096]{1,0:T(8,128)S(1)}, f32[32,4096]{1,0:T(8,128)}, u32[]{:S(2)}) copy-start(f32[32,4096]{1,0:T(8,128)} %fusion.53) | copy-start | bytes 1572868
  46.6 7.1 %copy-start.33 = (f32[32]{0:T(128)}, f32[32]{0:T(128)S(1)}, u32[]{:S(2)}) copy-start(f32[32]{0:T(128)S(1)} %add_rsqrt_fusion.1) | copy-start | bytes 388
  46.7 7.0 %collective-permute-start = (f32[256,128]{0,1:T(8,128)S(1)}, f32[256,128]{0,1:T(8,128)S(1)}, u32[]{:S(2)}, u32[]{:S(2)}) collective-permute-start(f32[256,128]{0,1:T(8,128)S(1)} %fusion.88), channel_id=1, source_target_pairs={{0,1},{1,0},{2,3},{3,2},{4,5},{5,4},{6,7},{7,6},{8,9},{9,8},{10,11... | collective-permute-start | bytes 393224 | tf_op jit(solution)/shard_map/ppermute | solution.py:17
  48.9 4.9 %copy-start.19 = (f32[32,64]{1,0:T(8,128)}, f32[32,64]{1,0:T(8,128)S(1)}, u32[]{:S(2)}) copy-start(f32[32,64]{1,0:T(8,128)S(1)} %get-tuple-element.41) | copy-start | bytes 24580
  49.0 7.5 %copy-start.24 = (bf16[32,128]{1,0:T(8,128)(2,1)}, bf16[32,128]{1,0:T(8,128)(2,1)S(1)}, u32[]{:S(2)}) copy-start(bf16[32,128]{1,0:T(8,128)(2,1)S(1)} %fusion.56) | copy-start | bytes 24580
  53.7 2.8 %copy-start.22 = (f32[256]{0:T(256)}, f32[256]{0:T(256)S(1)}, u32[]{:S(2)}) copy-start(f32[256]{0:T(256)S(1)} %add_rsqrt_fusion) | copy-start | bytes 3076
  54.3 0.6 copy-start.16
  55.2 13.6 %copy-start.9 = (f32[32,256]{1,0:T(8,128)}, f32[32,256]{1,0:T(8,128)S(1)}, u32[]{:S(2)}) copy-start(f32[32,256]{1,0:T(8,128)S(1)} %get-tuple-element.36) | copy-start | bytes 98308
  55.2 13.6 %copy-start.39 = (f32[32]{0:T(128)}, f32[32]{0:T(128)S(1)}, u32[]{:S(2)}) copy-start(f32[32]{0:T(128)S(1)} %get-tuple-element.35) | copy-start | bytes 388
  55.3 5.6 %copy-start.14 = (bf16[256,128]{0,1:T(8,128)(2,1)}, bf16[256,128]{0,1:T(8,128)(2,1)S(1)}, u32[]{:S(2)}) copy-start(bf16[256,128]{0,1:T(8,128)(2,1)S(1)} %select_convert_fusion) | copy-start | bytes 196612
  56.5 12.2 %all-to-all-start.1 = ((bf16[16,32,256]{2,1,0:T(8,128)(2,1)}), bf16[16,32,256]{2,1,0:T(8,128)(2,1)S(1)}, u32[]{:S(2)}, u32[]{:S(2)}) async-start(bf16[16,32,256]{2,1,0:T(8,128)(2,1)} %bitcast.78), calls=%async_computation.1 | async-start | bytes 524288 | tf_op jit(solution)/shard_map/all_to_all | solution.py:64
  60.8 54.2 %copy-start.27 = (f32[256]{0:T(256)}, f32[256]{0:T(256)S(1)}, u32[]{:S(2)}) copy-start(f32[256]{0:T(256)S(1)} %dynamic_slice.30) | copy-start | bytes 3076
  68.8 44.9 %copy-start.11 = (f32[32,256]{1,0:T(8,128)}, f32[32,256]{1,0:T(8,128)S(1)}, u32[]{:S(2)}) copy-start(f32[32,256]{1,0:T(8,128)S(1)} %convert_reduce_fusion.1) | copy-start | bytes 98308
  113.7 0.7 copy-start.5
  115.9 5.8 %copy-start.48 = (s32[256]{0:T(256)S(1)}, s32[256]{0:T(256)}, u32[]{:S(2)}) copy-start(s32[256]{0:T(256)} %param.13) | copy-start | bytes 3076
  115.9 6.5 %copy-start.46 = (s32[256,7]{0,1:T(8,128)S(1)}, s32[256,7]{0,1:T(8,128)}, u32[]{:S(2)}) copy-start(s32[256,7]{0,1:T(8,128)} %param.14) | copy-start | bytes 21508
  118.1 21.0 %all-to-all-start.3 = ((f32[16,104,128]{2,1,0:T(8,128)}), f32[16,104,128]{2,1,0:T(8,128)S(1)}, u32[]{:S(2)}, u32[]{:S(2)}) async-start(f32[16,104,128]{2,1,0:T(8,128)} %pad_maximum_fusion), calls=%async_computation.3 | async-start | bytes 1703936 | tf_op jit(solution)/shard_map/all_to_all | solution.py:64
  121.8 0.7 copy-start.45
  122.7 1.5 copy-start.21
  123.5 0.6 copy-start.29
  139.1 11.7 %copy-start.6 = (bf16[256,256]{1,0:T(8,128)(2,1)S(1)}, bf16[256,256]{1,0:T(8,128)(2,1)}, u32[]{:S(2)}) copy-start(bf16[256,256]{1,0:T(8,128)(2,1)} %copy-done.5) | copy-start | bytes 393220
  145.3 16.3 %all-to-all-start.4 = ((bf16[16,128,128]{2,1,0:T(8,128)(2,1)}), bf16[16,128,128]{2,1,0:T(8,128)(2,1)}, u32[]{:S(2)}, u32[]{:S(2)}) async-start(bf16[16,128,128]{2,1,0:T(8,128)(2,1)} %broadcast_in_dim.40), calls=%async_computation.4 | async-start | bytes 1048576 | tf_op jit(solution)/shard_map/all_to_all | solution.py:64
  162.6 0.6 copy-start.13
  165.3 1.5 copy-start.26
  165.3 3.2 %copy-start.49 = (f32[8]{0:T(128)S(1)}, f32[8]{0:T(128)}, u32[]{:S(2)}) copy-start(f32[8]{0:T(128)} %dynamic_slice.31) | copy-start | bytes 100
  165.3 3.2 %copy-start.50 = (f32[24]{0:T(128)S(1)}, f32[24]{0:T(128)}, u32[]{:S(2)}) copy-start(f32[24]{0:T(128)} %dynamic_slice.32) | copy-start | bytes 292
  165.3 3.3 %copy-start.12 = (f32[32,256]{1,0:T(8,128)S(1)}, f32[32,256]{1,0:T(8,128)}, u32[]{:S(2)}) copy-start(f32[32,256]{1,0:T(8,128)} %copy-done.11) | copy-start | bytes 98308
  165.3 3.3 %copy-start.28 = (f32[256]{0:T(256)S(1)}, f32[256]{0:T(256)}, u32[]{:S(2)}) copy-start(f32[256]{0:T(256)} %copy-done.27) | copy-start | bytes 3076
  165.6 15.1 %copy-start.10 = (f32[32,256]{1,0:T(8,128)S(1)}, f32[32,256]{1,0:T(8,128)}, u32[]{:S(2)}) copy-start(f32[32,256]{1,0:T(8,128)} %copy-done.9) | copy-start | bytes 98308
  166.8 13.9 %copy-start.15 = (bf16[256,128]{0,1:T(8,128)(2,1)S(1)}, bf16[256,128]{0,1:T(8,128)(2,1)}, u32[]{:S(2)}) copy-start(bf16[256,128]{0,1:T(8,128)(2,1)} %copy-done.14) | copy-start | bytes 196612
  166.8 13.9 %copy-start.40 = (f32[32]{0:T(128)S(1)}, f32[32]{0:T(128)}, u32[]{:S(2)}) copy-start(f32[32]{0:T(128)} %copy-done.39) | copy-start | bytes 388
  166.8 14.3 %copy-start.17 = (bf16[256,128]{0,1:T(8,128)(2,1)S(1)}, bf16[256,128]{0,1:T(8,128)(2,1)}, u32[]{:S(2)}) copy-start(bf16[256,128]{0,1:T(8,128)(2,1)} %copy-done.16) | copy-start | bytes 196612
  166.8 14.4 %copy-start.25 = (bf16[32,128]{1,0:T(8,128)(2,1)S(1)}, bf16[32,128]{1,0:T(8,128)(2,1)}, u32[]{:S(2)}) copy-start(bf16[32,128]{1,0:T(8,128)(2,1)} %copy-done.24) | copy-start | bytes 24580
  166.8 14.7 %copy-start.20 = (f32[32,64]{1,0:T(8,128)S(1)}, f32[32,64]{1,0:T(8,128)}, u32[]{:S(2)}) copy-start(f32[32,64]{1,0:T(8,128)} %copy-done.19) | copy-start | bytes 24580
  166.8 14.7 %copy-start.34 = (f32[32]{0:T(128)S(1)}, f32[32]{0:T(128)}, u32[]{:S(2)}) copy-start(f32[32]{0:T(128)} %copy-done.33) | copy-start | bytes 388
  166.8 14.7 %copy-start.36 = (f32[128]{0:T(128)S(1)}, f32[128]{0:T(128)}, u32[]{:S(2)}) copy-start(f32[128]{0:T(128)} %param.18) | copy-start | bytes 1540
  166.8 15.0 %copy-start.8 = (f32[256,64]{0,1:T(8,128)S(1)}, f32[256,64]{0,1:T(8,128)}, u32[]{:S(2)}) copy-start(f32[256,64]{0,1:T(8,128)} %copy-done.7) | copy-start | bytes 196612
  166.8 15.0 %copy-start.23 = (f32[256]{0:T(256)S(1)}, f32[256]{0:T(256)}, u32[]{:S(2)}) copy-start(f32[256]{0:T(256)} %copy-done.22) | copy-start | bytes 3076
  166.9 15.0 %copy-start.42 = (f32[128]{0:T(128)S(1)}, f32[128]{0:T(128)}, u32[]{:S(2)}) copy-start(f32[128]{0:T(128)} %param.19) | copy-start | bytes 1540
  180.2 4.9 %copy-start.31 = (s32[32]{0:T(128)S(1)}, s32[32]{0:T(128)}, u32[]{:S(2)}) copy-start(s32[32]{0:T(128)} %copy-done.30) | copy-start | bytes 388
  182.6 6.9 %collective-permute-start.1 = (f32[256,128]{0,1:T(8,128)S(1)}, f32[256,128]{0,1:T(8,128)S(1)}, u32[]{:S(2)}, u32[]{:S(2)}) collective-permute-start(f32[256,128]{0,1:T(8,128)S(1)} %get-tuple-element.39), channel_id=1, source_target_pairs={{0,1},{1,0},{2,3},{3,2},{4,5},{5,4},{6,7},{7,6},{8,9},{9,8},{10,11... | collective-permute-start | bytes 393224 | tf_op jit(solution)/shard_map/ppermute | solution.py:17
  193.8 31.7 %all-to-all-start.6 = ((bf16[16,16,4096]{2,1,0:T(8,128)(2,1)}), bf16[16,16,4096]{2,1,0:T(8,128)(2,1)S(1)}, u32[]{:S(2)}, u32[]{:S(2)}) async-start(bf16[16,16,4096]{2,1,0:T(8,128)(2,1)} %bitcast.17), calls=%async_computation.6 | async-start | bytes 4194304 | tf_op jit(solution)/shard_map/all_to_all | solution.py:64
  197.5 28.3 %copy-start.3 = (bf16[16,4096]{1,0:T(8,128)(2,1)S(1)}, bf16[16,4096]{1,0:T(8,128)(2,1)}, u32[]{:S(2)}) copy-start(bf16[16,4096]{1,0:T(8,128)(2,1)} %param.11) | copy-start | bytes 393220
  197.5 28.3 %copy-start.18 = (f32[4096]{0:T(1024)S(1)}, f32[4096]{0:T(1024)}, u32[]{:S(2)}) copy-start(f32[4096]{0:T(1024)} %param.15) | copy-start | bytes 49156
  225.5 0.6 copy-start.38
  225.5 0.8 copy-start.32
  225.5 0.8 copy-start.44
